TPU v7x, 32 devices: a whole 2x2x4 slice. The times are simulated.
32 devices in a mesh: section: 8 (over z, x), tensor: 4 (over y, core).
Axes of the slice: x: 2, y: 2, z: 4, core: 2. Of those that a mesh axis runs over, the one named last changes fastest.
Arguments:
- tree_queries: bfloat16 [8, 32, 4, 16384], P('section', 'tensor'), may hold values from -8 to 8
- tree_kv: bfloat16 [8, 32, 4, 2, 1024], P('section', 'tensor'), may hold values from -8 to 8
- cache_kv: bfloat16 [8, 32, 96, 2, 1024], P('section', 'tensor'), may hold values from -8 to 8
- residual: bfloat16 [8, 32, 4, 16384], P('section', 'tensor'), may hold values from -24 to 24
- cache_lengths: int32 [32], P('tensor'), may hold values from 12 to 96
- tree_parents: int32 [32, 4], P('tensor'), may hold values from -1 to 2, as said below
- accepted: int32 [32], P('tensor'), may hold values from 0 to 4
- merging_weight: bfloat16 [3, 16384, 16384], P(None, 'section', 'tensor')
- merging_gain: bfloat16 [16384], P('tensor'), may hold values from 0.25 to 1.75
Outputs:
- verified: bfloat16 [8, 32, 4, 16384], P('section', 'tensor')
- draft_input: bfloat16 [32, 4, 16384], P('section', None, 'tensor')
Inputs may be any that keep to these rules, and one draw needn't show every extreme that they name: tree_parents[r, 0] = -1, and for t >= 1 tree_parents[r, t] lies in 0 .. t - 1.
All inputs are finite; a program needn't handle non-finite values.
Results may differ from a plain program's by a relative error of at most 0.005.
Values may be sent and summed in bfloat16 or wider, within the bound.
A program may use at most 128 MiB of HBM per device.

v0:
```python
import jax
import jax.numpy as jnp
from jax import lax
from jax.sharding import PartitionSpec as P

D = 16384
HEADS = 128
KV_HEADS = 8
HEAD_DIM = 128


def ancestors(parents):
    row_count, tokens = parents.shape
    identity = jnp.eye(tokens, dtype=jnp.float32)
    token_ids = jnp.arange(tokens, dtype=jnp.int32)
    lineage_rows = [jnp.broadcast_to(identity[0], (row_count, tokens))]
    for token_index in range(1, tokens):
        parent_hot = (parents[:, token_index][:, None] == token_ids[None, :]).astype(jnp.float32)
        earlier = jnp.stack(lineage_rows, axis=1)
        inherited = jnp.einsum("ru,ruv->rv", parent_hot[:, :token_index], earlier)
        lineage_rows.append(jnp.maximum(inherited, identity[token_index][None, :]))
    return jnp.stack(lineage_rows, axis=1)


def attend(queries, tree_kv, cache_kv, residual, lengths, lineage):
    row_count, tokens, feature_width = queries.shape
    group_size = HEADS // KV_HEADS
    factor = HEAD_DIM ** (-0.5)
    highest = lax.Precision.HIGHEST
    key_span = 16
    grouped = queries.reshape(row_count, tokens, KV_HEADS, group_size, HEAD_DIM)
    own_keys = tree_kv[:, :, 0].reshape(row_count, tokens, KV_HEADS, HEAD_DIM)
    own_values = tree_kv[:, :, 1].reshape(row_count, tokens, KV_HEADS, HEAD_DIM).astype(jnp.float32)
    tree_scores = (
        jnp.einsum("rtkgd,rukd->rtkgu", grouped, own_keys, preferred_element_type=jnp.float32)
        * factor
    )
    tree_scores = jnp.where(lineage[:, :, None, None, :] > 0.5, tree_scores, -jnp.inf)
    row_max = jnp.max(tree_scores, axis=-1)
    weights = jnp.exp(tree_scores - row_max[..., None])
    weight_sum = jnp.sum(weights, axis=-1)
    weighted = jnp.einsum("rtkgu,rukd->rtkgd", weights, own_values, precision=highest)
    block_count = (jnp.max(lengths) + key_span - 1) // key_span

    def visit(block_index, state_now):
        old_max, old_sum, old_weighted = state_now
        window = lax.dynamic_slice_in_dim(cache_kv, block_index * key_span, key_span, 1)
        block_keys = window[:, :, 0].reshape(row_count, key_span, KV_HEADS, HEAD_DIM)
        block_values = (
            window[:, :, 1].reshape(row_count, key_span, KV_HEADS, HEAD_DIM).astype(jnp.float32)
        )
        scores = (
            jnp.einsum("rtkgd,rskd->rtkgs", grouped, block_keys, preferred_element_type=jnp.float32)
            * factor
        )
        positions = block_index * key_span + jnp.arange(key_span, dtype=jnp.int32)
        in_cache = positions[None, :] < lengths[:, None]
        scores = jnp.where(in_cache[:, None, None, None, :], scores, -jnp.inf)
        new_max = jnp.maximum(old_max, jnp.max(scores, axis=-1))
        rescale = jnp.exp(old_max - new_max)
        block_weights = jnp.exp(scores - new_max[..., None])
        new_sum = old_sum * rescale + jnp.sum(block_weights, axis=-1)
        new_weighted = old_weighted * rescale[..., None] + jnp.einsum(
            "rtkgs,rskd->rtkgd", block_weights, block_values, precision=highest
        )
        return (new_max, new_sum, new_weighted)

    row_max, weight_sum, weighted = lax.fori_loop(
        0, block_count, visit, (row_max, weight_sum, weighted)
    )
    attention = (weighted / weight_sum[..., None]).reshape(row_count, tokens, feature_width)
    return (residual.astype(jnp.float32) + attention).astype(jnp.bfloat16)


def feature_block(masked, section_index, section_count, capture_roots, block_width):
    row_total = masked.shape[0] * masked.shape[1]
    flat_rows = masked.reshape(row_total, -1)
    nothing = jnp.zeros((), jnp.bfloat16)
    is_root = (
        (section_index == capture_roots[0])
        | (section_index == capture_roots[1])
        | (section_index == capture_roots[2])
    )
    outgoing = jnp.where(is_root, flat_rows, nothing).reshape(row_total, section_count, block_width)
    incoming = lax.all_to_all(outgoing, "section", split_axis=1, concat_axis=1, tiled=True)
    return jnp.concatenate([incoming[:, root_section] for root_section in capture_roots], axis=-1)


def local(
    tree_queries,
    tree_kv,
    cache_kv,
    residual,
    cache_lengths,
    tree_parents,
    accepted,
    merging_weight,
    merging_gain,
):
    section_count = lax.axis_size("section")
    section_index = lax.axis_index("section")
    tokens = tree_queries.shape[2]
    block_width = merging_weight.shape[1]
    local_weight = merging_weight.reshape(3 * block_width, merging_weight.shape[2])
    lineage = ancestors(tree_parents)
    capture_roots = (0, section_count // 2, section_count - 1)
    accepted_mask = (jnp.arange(tokens, dtype=jnp.int32)[None, :] < accepted[:, None])[:, :, None]
    nothing = jnp.zeros((), jnp.bfloat16)
    verified = attend(tree_queries[0], tree_kv[0], cache_kv[0], residual[0], cache_lengths, lineage)
    masked = jnp.where(accepted_mask, verified, nothing)
    column_block = feature_block(masked, section_index, section_count, capture_roots, block_width)
    gathered = lax.all_gather(column_block, "tensor", axis=0, tiled=True)
    own_count = gathered.shape[0] // section_count
    own_rows = lax.psum_scatter(
        jnp.dot(gathered, local_weight, preferred_element_type=jnp.float32),
        "section",
        scatter_dimension=0,
        tiled=True,
    )
    squares = lax.psum(jnp.sum(own_rows * own_rows, axis=1), "tensor")
    inverse_rms = lax.rsqrt(squares / D + 1e-05)
    normed = own_rows * inverse_rms[:, None] * merging_gain.astype(jnp.float32)[None, :]
    draft_input = normed.astype(jnp.bfloat16).reshape(own_count // tokens, tokens, -1)
    return (verified[None], draft_input)


def solution(mesh):
    return jax.shard_map(
        local,
        mesh=mesh,
        in_specs=(
            P("section", "tensor", None, None),
            P("section", "tensor", None, None, None),
            P("section", "tensor", None, None, None),
            P("section", "tensor", None, None),
            P("tensor"),
            P("tensor", None),
            P("tensor"),
            P(None, "section", "tensor"),
            P("tensor"),
        ),
        out_specs=(P("section", "tensor", None, None), P("section", None, "tensor")),
        check_vma=False,
    )
```

profile of v0, /device:TPU:0, one launch (start us, length us, event | category | flops | bytes accessed | tf_op | source)
XLA Modules:
  0.0 226.6 jit_solution(3225477163077049415)
XLA Ops:
  7.2 1.3 reduce_max.28
  10.7 2.1 reshape.135
  13.9 2.7 %fusion.25 = (f32[8,4,8,16]{3,1,2,0:T(4,128)S(1)}, f32[8,4,8,16,4]{3,4,1,2,0:T(4,128)S(1)}) fusion(bf16[8,4,8,16,128]{4,3,2,1,0:T(8,128)(2,1)S(1)} %reshape.135, bf16[8,4,8,128,1]{3,2,1,0,4:T(8,128)(2,1)S(1)} %bitcast.132, pred[8,4,4]{2,1,0:T(4,128)(4,1)S(1)} %copy.62), kind=kOutput, calls=%fused_computation.73 | convolution fusion | flops 4239360 | bytes 1196160 | tf_op jit(solution)/shard_map/rtkgd,rukd->rtkgu/dot_general | solution.py:35
  17.0 1.9 convolution_bitcast_fusion
  19.0 4.6 %copy.127 = bf16[1,8,96,2,1024]{4,2,1,3,0:T(8,128)(2,1)} copy(bf16[1,8,96,2,1024]{4,3,2,1,0:T(2,128)(2,1)} %param.13) | data formatting | bytes 6291456 | tf_op args[2]
  23.5 48.7 %while.14 = (s32[]{:T(128)}, f32[8,4,8,16]{3,1,2,0:T(4,128)S(1)}, f32[8,4,8,16]{3,1,2,0:T(4,128)S(1)}, f32[8,4,8,16,128]{4,3,1,2,0:T(8,128)S(1)}, s32[]{:T(128)}...) while((s32[]{:T(128)}, f32[8,4,8,16]{3,1,2,0:T(4,128)S(1)}, ...), condition=%wide.region_6.7_spmd, body=%wide.region_3.6_spmd.sunk | while | flops 119152792 | bytes 9962339 | solution.py:68
  24.8 2.6 %bitcast_reduce_fusion.2 = (f32[8,4,8,16]{3,1,2,0:T(4,128)S(1)}, f32[8,8,16,4,16]{4,2,3,1,0:T(8,128)S(1)}) fusion(pred[8,16]{1,0:T(8,128)(4,1)S(1)} %broadcast_compare_fusion.2, bf16[8,4,8,16,128]{4,3,1,2,0:T(8,128)(2,1)S(1)} %get-tuple-element.217, bf16[8,16,8,128,1]{3,2,1,0,4:T(8,128)(2,1)S(1)} %bitcast_bitcast_fusion.4), kind=kOutput, calls=%fused_computation.2.clone.1 | convolution fusion | flops 16969728 | bytes 1589376 | tf_op jit(solution)/shard_map/while/body/rtkgd,rskd->rtkgs/dot_general | solution.py:53
  28.5 3.1 %bitcast_add_fusion.2 = f32[8,4,8,16,128]{4,3,1,2,0:T(8,128)S(1)} fusion(f32[8,4,8,16,128]{4,3,1,2,0:T(8,128)S(1)} %get-tuple-element.200, f32[8,8,16,4,16]{4,2,3,1,0:T(8,128)S(1)} %get-tuple-element.180, f32[8,4,8,16]{3,1,2,0:T(4,128)S(1)} %bitcast.125, f32[8,4,8,16]{3,1,2,0:T(4,128)S(1)} %max.49, pred[8,16]{1,0:T(8,128)(4,1)S(1)} %broadcast_compare_fusion.2, ...), kind=kOutput, calls=%fused_computation.clone.1 | convolution fusion | flops 101908480 | bytes 4751488 | tf_op jit(solution)/shard_map/while/body/rtkgs,rskd->rtkgd/dot_general | solution.py:63
  31.7 1.1 constant_dynamic-slice_fusion.3
  32.9 2.6 %bitcast_reduce_fusion.2 = (f32[8,4,8,16]{3,1,2,0:T(4,128)S(1)}, f32[8,8,16,4,16]{4,2,3,1,0:T(8,128)S(1)}) fusion(pred[8,16]{1,0:T(8,128)(4,1)S(1)} %broadcast_compare_fusion.2, bf16[8,4,8,16,128]{4,3,1,2,0:T(8,128)(2,1)S(1)} %get-tuple-element.217, bf16[8,16,8,128,1]{3,2,1,0,4:T(8,128)(2,1)S(1)} %bitcast_bitcast_fusion.4), kind=kOutput, calls=%fused_computation.2.clone.1 | convolution fusion | flops 16969728 | bytes 1589376 | tf_op jit(solution)/shard_map/while/body/rtkgd,rskd->rtkgs/dot_general | solution.py:53
  36.6 3.1 %bitcast_add_fusion.2 = f32[8,4,8,16,128]{4,3,1,2,0:T(8,128)S(1)} fusion(f32[8,4,8,16,128]{4,3,1,2,0:T(8,128)S(1)} %get-tuple-element.200, f32[8,8,16,4,16]{4,2,3,1,0:T(8,128)S(1)} %get-tuple-element.180, f32[8,4,8,16]{3,1,2,0:T(4,128)S(1)} %bitcast.125, f32[8,4,8,16]{3,1,2,0:T(4,128)S(1)} %max.49, pred[8,16]{1,0:T(8,128)(4,1)S(1)} %broadcast_compare_fusion.2, ...), kind=kOutput, calls=%fused_computation.clone.1 | convolution fusion | flops 101908480 | bytes 4751488 | tf_op jit(solution)/shard_map/while/body/rtkgs,rskd->rtkgd/dot_general | solution.py:63
  39.8 1.1 constant_dynamic-slice_fusion.3
  41.0 2.6 %bitcast_reduce_fusion.2 = (f32[8,4,8,16]{3,1,2,0:T(4,128)S(1)}, f32[8,8,16,4,16]{4,2,3,1,0:T(8,128)S(1)}) fusion(pred[8,16]{1,0:T(8,128)(4,1)S(1)} %broadcast_compare_fusion.2, bf16[8,4,8,16,128]{4,3,1,2,0:T(8,128)(2,1)S(1)} %get-tuple-element.217, bf16[8,16,8,128,1]{3,2,1,0,4:T(8,128)(2,1)S(1)} %bitcast_bitcast_fusion.4), kind=kOutput, calls=%fused_computation.2.clone.1 | convolution fusion | flops 16969728 | bytes 1589376 | tf_op jit(solution)/shard_map/while/body/rtkgd,rskd->rtkgs/dot_general | solution.py:53
  44.8 3.1 %bitcast_add_fusion.2 = f32[8,4,8,16,128]{4,3,1,2,0:T(8,128)S(1)} fusion(f32[8,4,8,16,128]{4,3,1,2,0:T(8,128)S(1)} %get-tuple-element.200, f32[8,8,16,4,16]{4,2,3,1,0:T(8,128)S(1)} %get-tuple-element.180, f32[8,4,8,16]{3,1,2,0:T(4,128)S(1)} %bitcast.125, f32[8,4,8,16]{3,1,2,0:T(4,128)S(1)} %max.49, pred[8,16]{1,0:T(8,128)(4,1)S(1)} %broadcast_compare_fusion.2, ...), kind=kOutput, calls=%fused_computation.clone.1 | convolution fusion | flops 101908480 | bytes 4751488 | tf_op jit(solution)/shard_map/while/body/rtkgs,rskd->rtkgd/dot_general | solution.py:63
  47.9 1.1 constant_dynamic-slice_fusion.3
  49.1 2.6 %bitcast_reduce_fusion.2 = (f32[8,4,8,16]{3,1,2,0:T(4,128)S(1)}, f32[8,8,16,4,16]{4,2,3,1,0:T(8,128)S(1)}) fusion(pred[8,16]{1,0:T(8,128)(4,1)S(1)} %broadcast_compare_fusion.2, bf16[8,4,8,16,128]{4,3,1,2,0:T(8,128)(2,1)S(1)} %get-tuple-element.217, bf16[8,16,8,128,1]{3,2,1,0,4:T(8,128)(2,1)S(1)} %bitcast_bitcast_fusion.4), kind=kOutput, calls=%fused_computation.2.clone.1 | convolution fusion | flops 16969728 | bytes 1589376 | tf_op jit(solution)/shard_map/while/body/rtkgd,rskd->rtkgs/dot_general | solution.py:53
  52.9 3.1 %bitcast_add_fusion.2 = f32[8,4,8,16,128]{4,3,1,2,0:T(8,128)S(1)} fusion(f32[8,4,8,16,128]{4,3,1,2,0:T(8,128)S(1)} %get-tuple-element.200, f32[8,8,16,4,16]{4,2,3,1,0:T(8,128)S(1)} %get-tuple-element.180, f32[8,4,8,16]{3,1,2,0:T(4,128)S(1)} %bitcast.125, f32[8,4,8,16]{3,1,2,0:T(4,128)S(1)} %max.49, pred[8,16]{1,0:T(8,128)(4,1)S(1)} %broadcast_compare_fusion.2, ...), kind=kOutput, calls=%fused_computation.clone.1 | convolution fusion | flops 101908480 | bytes 4751488 | tf_op jit(solution)/shard_map/while/body/rtkgs,rskd->rtkgd/dot_general | solution.py:63
  57.3 2.6 %bitcast_reduce_fusion.2 = (f32[8,4,8,16]{3,1,2,0:T(4,128)S(1)}, f32[8,8,16,4,16]{4,2,3,1,0:T(8,128)S(1)}) fusion(pred[8,16]{1,0:T(8,128)(4,1)S(1)} %broadcast_compare_fusion.2, bf16[8,4,8,16,128]{4,3,1,2,0:T(8,128)(2,1)S(1)} %get-tuple-element.217, bf16[8,16,8,128,1]{3,2,1,0,4:T(8,128)(2,1)S(1)} %bitcast_bitcast_fusion.4), kind=kOutput, calls=%fused_computation.2.clone.1 | convolution fusion | flops 16969728 | bytes 1589376 | tf_op jit(solution)/shard_map/while/body/rtkgd,rskd->rtkgs/dot_general | solution.py:53
  61.0 3.1 %bitcast_add_fusion.2 = f32[8,4,8,16,128]{4,3,1,2,0:T(8,128)S(1)} fusion(f32[8,4,8,16,128]{4,3,1,2,0:T(8,128)S(1)} %get-tuple-element.200, f32[8,8,16,4,16]{4,2,3,1,0:T(8,128)S(1)} %get-tuple-element.180, f32[8,4,8,16]{3,1,2,0:T(4,128)S(1)} %bitcast.125, f32[8,4,8,16]{3,1,2,0:T(4,128)S(1)} %max.49, pred[8,16]{1,0:T(8,128)(4,1)S(1)} %broadcast_compare_fusion.2, ...), kind=kOutput, calls=%fused_computation.clone.1 | convolution fusion | flops 101908480 | bytes 4751488 | tf_op jit(solution)/shard_map/while/body/rtkgs,rskd->rtkgd/dot_general | solution.py:63
  65.4 2.6 %bitcast_reduce_fusion.2 = (f32[8,4,8,16]{3,1,2,0:T(4,128)S(1)}, f32[8,8,16,4,16]{4,2,3,1,0:T(8,128)S(1)}) fusion(pred[8,16]{1,0:T(8,128)(4,1)S(1)} %broadcast_compare_fusion.2, bf16[8,4,8,16,128]{4,3,1,2,0:T(8,128)(2,1)S(1)} %get-tuple-element.217, bf16[8,16,8,128,1]{3,2,1,0,4:T(8,128)(2,1)S(1)} %bitcast_bitcast_fusion.4), kind=kOutput, calls=%fused_computation.2.clone.1 | convolution fusion | flops 16969728 | bytes 1589376 | tf_op jit(solution)/shard_map/while/body/rtkgd,rskd->rtkgs/dot_general | solution.py:53
  69.1 3.1 %bitcast_add_fusion.2 = f32[8,4,8,16,128]{4,3,1,2,0:T(8,128)S(1)} fusion(f32[8,4,8,16,128]{4,3,1,2,0:T(8,128)S(1)} %get-tuple-element.200, f32[8,8,16,4,16]{4,2,3,1,0:T(8,128)S(1)} %get-tuple-element.180, f32[8,4,8,16]{3,1,2,0:T(4,128)S(1)} %bitcast.125, f32[8,4,8,16]{3,1,2,0:T(4,128)S(1)} %max.49, pred[8,16]{1,0:T(8,128)(4,1)S(1)} %broadcast_compare_fusion.2, ...), kind=kOutput, calls=%fused_computation.clone.1 | convolution fusion | flops 101908480 | bytes 4751488 | tf_op jit(solution)/shard_map/while/body/rtkgs,rskd->rtkgd/dot_general | solution.py:63
  73.2 1.5 reshape.121
  74.7 1.6 reshape.125
  76.5 2.5 %fusion.15 = bf16[32,8,2048]{2,1,0:T(8,128)(2,1)S(1)} fusion(f32[32,8,2048]{2,1,0:T(8,128)} %reshape.125, f32[32,8,2048]{2,1,0:T(8,128)} %reshape.121, pred[32]{0:T(512)(128)(4,1)S(1)} %lt.43, pred[]{:T(512)S(6)} %or.7), kind=kLoop, calls=%fused_computation.31 | loop fusion | flops 2097152 | bytes 5242913 | tf_op jit(solution)/shard_map/jit(_where)/select_n | solution.py:84
  79.6 23.0 %all_to_all.5 = bf16[32,8,2048]{2,0,1:T(8,128)(2,1)S(1)} all-to-all(bf16[32,8,2048]{2,0,1:T(8,128)(2,1)S(1)} %copy.73), channel_id=1, replica_groups=mesh['section'=8,'tensor'=4] {'section'}, dimensions={1} | all-to-all | bytes 2097152 | tf_op jit(solution)/shard_map/all_to_all | solution.py:85
  103.7 18.6 %all-gather.2.cloned.1.call-done = bf16[128,6144]{1,0:T(8,128)(2,1)} async-done(((bf16[32,6144]{1,0:T(8,128)(2,1)}), bf16[128,6144]{1,0:T(8,128)(2,1)}) %all-gather.2.cloned.1.call-update) | async-done | bytes 1572880 | tf_op jit(solution)/shard_map/all_gather | solution.py:112
  122.3 20.6 %fusion.26 = f32[128,4096]{1,0:T(8,128)} fusion(bf16[128,6144]{1,0:T(8,128)(2,1)} %all-gather.2.cloned.1.call-done, bf16[6144,4096]{1,0:T(8,128)(2,1)} %bitcast.118), kind=kOutput, calls=%fused_computation.74 | convolution fusion | flops 6442450944 | bytes 54001664 | tf_op jit(solution)/shard_map/dot_general | solution.py:115
  142.9 1.9 reshape.120
  144.8 3.1 %add_convert_fusion.1 = bf16[1,8,4,16384]{3,2,1,0:T(4,128)(2,1)} fusion(f32[1,8,4,16384]{3,2,1,0:T(4,128)} %reshape.120, bf16[1,8,4,16384]{3,2,1,0:T(4,128)(2,1)S(1)} %copy-done), kind=kLoop, calls=%fused_computation.25 | loop fusion | flops 1572864 | bytes 4194304 | tf_op jit(solution)/shard_map/convert_element_type | solution.py:72
  147.9 63.4 %reduce-scatter.2.cloned.1.call-done = f32[16,4096]{1,0:T(8,128)} async-done(((f32[128,4096]{1,0:T(8,128)}), f32[16,4096]{1,0:T(8,128)}) %reduce-scatter.2.cloned.1.call-update) | async-done | bytes 262160 | tf_op jit(solution)/shard_map/reduce_scatter | solution.py:114
  211.2 1.1 multiply_reduce_fusion
  212.3 5.7 %psum.7 = f32[16]{0:T(128)S(1)} all-reduce(f32[16]{0:T(128)S(1)} %multiply_reduce_fusion), channel_id=1, replica_groups=mesh['section'=8,'tensor'=4] {'tensor'}, use_global_device_ids=true, to_apply=%region_9.10 | all-reduce | flops 16 | bytes 128 | tf_op jit(solution)/shard_map/psum | solution.py:120
  (111 shorter events, 18.3 us)
Async XLA Ops:
  7.2 5.7 %copy-start.1 = (bf16[1,8,4,2,1024]{4,3,2,1,0:T(2,128)(2,1)S(1)}, bf16[1,8,4,2,1024]{4,3,2,1,0:T(2,128)(2,1)}, u32[]{:S(2)}) copy-start(bf16[1,8,4,2,1024]{4,3,2,1,0:T(2,128)(2,1)} %param.12) | copy-start | bytes 393220
  7.2 115.1 %all-gather.2.cloned.1.call-start = ((), (), s32[]{:S(2)}) async-start(), calls=%async_computation.2 | async-start | bytes 1966080 | tf_op jit(solution)/shard_map/all_gather | solution.py:112
  19.0 4.6 %copy-start.2 = (s32[8]{0:T(128)S(1)}, s32[8]{0:T(128)}, u32[]{:S(2)}) copy-start(s32[8]{0:T(128)} %param.15) | copy-start | bytes 100
  73.2 1.5 copy-start
  74.7 1.7 copy-start.4
  103.4 107.8 %reduce-scatter.2.cloned.1.call-start = ((), (), s32[]{:S(2)}) async-start(), calls=%async_computation.3 | async-start | bytes 2359296 | tf_op jit(solution)/shard_map/reduce_scatter | solution.py:114
  142.9 1.9 copy-start.3
Sparse Core Ops, SparseCore 0:
  103.5 18.6 all-gather.1
  143.0 68.2 reduce-scatter.1
where the time goes:
time: 228 us; the launch traced here: 227 us
  waiting for transfers between devices  82 us (36%)
  matrix products  59.3 us (26%)
  blocking collectives  28.7 us (13%)
  local copies, waits for them, and re-layouts  22.7 us (10%)
  other arithmetic  18.1 us (8%)
  between operations  14.9 us (7%)
    reduce_scatter x1, waiting for transfers between devices, local(): lax.psum_scatter(jnp.dot(gathered, local_weight, preferred_element_type=j...  63.4 us
    all_to_all x1, blocking collectives, feature_block(): lax.all_to_all(outgoing, 'section', split_axis=1, concat_axis=1, tiled=True)  23 us
    dot_general x1, matrix products, local(): jnp.dot(gathered, local_weight, preferred_element_type=jnp.float32)  20.6 us
    all_gather x1, waiting for transfers between devices, local(): gathered = lax.all_gather(column_block, 'tensor', axis=0, tiled=True)  18.6 us
    dot_general x6, matrix products, visit(): jnp.einsum('rtkgs,rskd->rtkgd', block_weights, block_values, precision=hi...  18.5 us
    dot_general x6, matrix products, visit(): jnp.einsum('rtkgd,rskd->rtkgs', grouped, block_keys, preferred_element_ty...  15.7 us
    slice x6, local copies, waits for them, and re-layouts, visit(): window[:, :, 1].reshape(row_count, key_span, KV_HEADS, HEAD_DIM)  6.45 us
    psum x1, blocking collectives, local(): squares = lax.psum(jnp.sum(own_rows * own_rows, axis=1), 'tensor')  5.66 us
  transfers between devices with their start and end apart: 2, of which 2 were waited for; matrix products, arithmetic and copies ran while one was open for 2% of the time, Pallas kernels for 0%

commit v1 on v0

v1 whole, which is shorter than its diff:
```python
import functools

import jax
import jax.numpy as jnp
from jax import lax
from jax.experimental import pallas as pl
from jax.experimental.pallas import tpu as pltpu
from jax.sharding import PartitionSpec as P

KV_HEADS = 8
HEAD_DIM = 128
MESH = pl.DeviceIdType.MESH
F32 = jnp.float32
BF16 = jnp.bfloat16


def attention_kernel(
    lengths_ref,
    parents_ref,
    accepted_ref,
    query_ref,
    cache_ref,
    tree_ref,
    residual_ref,
    verified_ref,
    captured_ref,
    kv_scr,
    head_scr,
    token_scr,
    captured_scr,
):
    row = pl.program_id(0)
    tokens = query_ref.shape[1]
    cached = cache_ref.shape[1]
    own = tree_ref.shape[1]
    span = kv_scr.shape[0]
    heads = query_ref.shape[2] // HEAD_DIM
    group = heads // KV_HEADS
    lines = group * tokens

    kv_scr[0:cached] = cache_ref[0]
    kv_scr[cached:span] = jnp.zeros((span - cached, kv_scr.shape[1]), BF16)
    kv_scr[cached : cached + own] = tree_ref[0]

    for head in range(heads):
        head_scr[head * tokens : (head + 1) * tokens, :] = query_ref[
            0, :, head * HEAD_DIM : (head + 1) * HEAD_DIM
        ].astype(F32)

    bits = [jnp.int32(1)]
    for token in range(1, tokens):
        parent = parents_ref[row, token]
        inherited = jnp.int32(0)
        for earlier in range(token):
            inherited = jnp.where(parent == earlier, bits[earlier], inherited)
        bits.append(inherited | (1 << token))
    token_id = lax.broadcasted_iota(jnp.int32, (lines, span), 0) % tokens
    column = lax.broadcasted_iota(jnp.int32, (lines, span), 1)
    line_bits = jnp.full((lines, span), bits[0], jnp.int32)
    for token in range(1, tokens):
        line_bits = jnp.where(token_id == token, bits[token], line_bits)
    own_index = jnp.clip((column - cached) // 2, 0, 31)
    in_tree = (
        (column >= cached)
        & (column < cached + own)
        & ((lax.shift_right_logical(line_bits, own_index) & 1) == 1)
    )
    in_cache = column < jnp.minimum(2 * lengths_ref[row], cached)
    allowed = (in_cache | in_tree) & (column % 2 == 0)

    factor = HEAD_DIM ** (-0.5)
    scores = []
    for kv in range(KV_HEADS):
        queries = head_scr[kv * lines : (kv + 1) * lines, :].astype(BF16)
        keys = kv_scr[:, kv * HEAD_DIM : (kv + 1) * HEAD_DIM]
        scores.append(
            lax.dot_general(
                queries, keys, (((1,), (1,)), ((), ())), preferred_element_type=F32
            )
        )
    for kv in range(KV_HEADS):
        score = jnp.where(allowed, scores[kv] * factor, -jnp.inf)
        weights = jnp.exp(score - jnp.max(score, axis=1, keepdims=True))
        total = jnp.sum(weights, axis=1, keepdims=True)
        shifted = pltpu.roll(weights, 1, 1).astype(BF16)
        weighted = jnp.dot(
            shifted,
            kv_scr[:, kv * HEAD_DIM : (kv + 1) * HEAD_DIM],
            preferred_element_type=F32,
        )
        head_scr[kv * lines : (kv + 1) * lines, :] = weighted / total

    keep = lax.broadcasted_iota(jnp.int32, (tokens, HEAD_DIM), 0) < accepted_ref[row]
    for head in range(heads):
        features = slice(head * HEAD_DIM, (head + 1) * HEAD_DIM)
        summed = (
            residual_ref[0, :, features].astype(F32)
            + head_scr[head * tokens : (head + 1) * tokens, :]
        )
        verified_ref[0, :, features] = summed.astype(BF16)
        token_scr[:, features] = jnp.where(keep, summed, 0.0)

    shared = captured_scr.shape[1] // tokens
    for place in range(shared):

        @pl.when(row % shared == place)
        def _(place=place):
            captured_scr[row // shared, place * tokens : (place + 1) * tokens, :] = token_scr[...]

    @pl.when(row == pl.num_programs(0) - 1)
    def _():
        captured_ref[...] = captured_scr[...].reshape(captured_ref.shape).astype(BF16)


def attend(queries, tree_kv, cache_kv, residual, lengths, parents, accepted):
    rows, tokens, width = queries.shape
    cached = 2 * cache_kv.shape[1]
    own = 2 * tokens
    span = -(-(cached + own) // 128) * 128
    kv_width = cache_kv.shape[3]
    row_block = lambda *shape: pl.BlockSpec((1,) + shape, lambda r: (r, 0, 0))
    scalars = pl.BlockSpec(memory_space=pltpu.SMEM)
    return pl.pallas_call(
        attention_kernel,
        grid=(rows,),
        out_shape=(
            jax.ShapeDtypeStruct((rows, tokens, width), BF16),
            jax.ShapeDtypeStruct((rows * tokens, width), BF16),
        ),
        in_specs=[
            scalars,
            scalars,
            scalars,
            row_block(tokens, width),
            row_block(cached, kv_width),
            row_block(own, kv_width),
            row_block(tokens, width),
        ],
        out_specs=(
            row_block(tokens, width),
            pl.BlockSpec((rows * tokens, width), lambda r: (0, 0)),
        ),
        scratch_shapes=[
            pltpu.VMEM((span, kv_width), BF16),
            pltpu.VMEM((width // HEAD_DIM * tokens, HEAD_DIM), F32),
            pltpu.VMEM((tokens, width), F32),
            pltpu.VMEM((rows * tokens // 8, 8, width), F32),
        ],
        compiler_params=pltpu.CompilerParams(vmem_limit_bytes=32 * 2**20),
        name="tree_attention",
    )(
        lengths,
        parents,
        accepted,
        queries,
        cache_kv.reshape(rows, cached, kv_width),
        tree_kv.reshape(rows, own, kv_width),
        residual,
    )


LAG = 2


def merge_kernel(
    sections,
    tensors,
    captured_ref,
    weight_ref,
    gain_ref,
    out_ref,
    weight_v,
    captured_v,
    sums,
    own,
    pair_out,
    pair_in,
    line_out,
    line_in,
    final,
    squares,
    weight_sem,
    local_sem,
    root_send,
    root_recv,
    row_send,
    row_recv,
    core_send,
    core_recv,
    pair_send,
    pair_recv,
    line_send,
    line_recv,
    square_send,
    square_recv,
):
    section = lax.axis_index("section")
    tensor = lax.axis_index("tensor")
    chunks, groups, block, width = weight_v.shape
    rows = captured_ref.shape[0]
    line = sections // 2
    out_rows = out_ref.shape[0]
    place, parity = section // 2, section % 2
    partner = section + 1 - 2 * parity
    other_core = tensor + 1 - 2 * (tensor % 2)
    roots = (0, sections // 2, sections - 1)

    def remote(src, dst, send, recv, to_section, to_tensor):
        return pltpu.make_async_remote_copy(
            src_ref=src,
            dst_ref=dst,
            send_sem=send,
            recv_sem=recv,
            device_id=(to_section, to_tensor),
            device_id_type=MESH,
        )

    def weight_copy(chunk):
        columns = pl.ds(pl.multiple_of(chunk * width, width), width)
        return pltpu.make_async_copy(
            weight_ref.at[:, :, columns], weight_v.at[chunk], weight_sem.at[chunk]
        )

    for chunk in range(chunks):
        weight_copy(chunk).start()

    barrier = pltpu.get_barrier_semaphore()
    for step in range(1, sections):
        pl.semaphore_signal(
            barrier, inc=1, device_id=((section + step) % sections, tensor), device_id_type=MESH
        )
    for step in range(1, tensors):
        pl.semaphore_signal(
            barrier, inc=1, device_id=(section, (tensor + step) % tensors), device_id_type=MESH
        )
    pl.semaphore_wait(barrier, sections + tensors - 2)

    def piece(group, owner):
        return captured_v.at[group, pl.ds(pl.multiple_of(owner * rows, rows), rows), :]

    def features(to_section):
        return captured_ref.at[:, pl.ds(pl.multiple_of(to_section * block, block), block)]

    def root_copy(group, step):
        to_section = (section + step) % sections
        return remote(
            features(to_section),
            piece(group, tensor),
            root_send.at[step - 1],
            root_recv.at[group],
            to_section,
            tensor,
        )

    def root_local(group):
        return pltpu.make_async_copy(features(section), piece(group, tensor), local_sem)

    for group, root in enumerate(roots):

        @pl.when(section == root)
        def _(group=group):
            for step in range(1, sections):
                root_copy(group, step).start()
            root_local(group).start()

    def row_copy(group, step):
        return remote(
            piece(group, tensor),
            piece(group, tensor),
            row_send.at[group, step - 1],
            row_recv.at[group, step - 1],
            section,
            (tensor + 2 * step) % tensors,
        )

    def core_copy(group, step):
        owner = (tensor + tensors - 2 * step) % tensors
        return remote(
            piece(group, owner),
            piece(group, owner),
            core_send.at[group, step],
            core_recv.at[group, step],
            section,
            other_core,
        )

    half = tensors // 2
    for group, root in enumerate(roots):

        @pl.when(section == root)
        def _(group=group):
            root_local(group).wait()

        @pl.when(section != root)
        def _(group=group):
            root_copy(group, 1).wait_recv()

        for step in range(1, half):
            row_copy(group, step).start()
        core_copy(group, 0).start()
    for group in range(groups):
        for step in range(1, half):
            row_copy(group, step).wait_recv()
            core_copy(group, step).start()
    for group in range(groups):
        for step in range(half):
            core_copy(group, step).wait_recv()

    def pair_copy(chunk):
        return remote(
            pair_out.at[chunk],
            pair_in.at[chunk],
            pair_send.at[chunk],
            pair_recv.at[chunk],
            partner,
            tensor,
        )

    def line_copy(chunk, step):
        to_place = (place + step) % line
        return remote(
            line_out.at[chunk, to_place],
            line_in.at[chunk, step - 1],
            line_send.at[chunk, step - 1],
            line_recv.at[chunk, step - 1],
            2 * to_place + parity,
            tensor,
        )

    def visit(turn, carry):
        @pl.when(turn < chunks)
        def _():
            chunk = turn
            weight_copy(chunk).wait()
            product = jnp.dot(captured_v[0], weight_v[chunk, 0], preferred_element_type=F32)
            for group in range(1, groups):
                product += jnp.dot(
                    captured_v[group], weight_v[chunk, group], preferred_element_type=F32
                )
            sums[...] = product.reshape(line, 2, out_rows, width)
            own[chunk] = sums[:, parity]
            pair_out[chunk] = sums[:, 1 - parity].astype(BF16)
            pair_copy(chunk).start()

        @pl.when(turn >= LAG)
        def _():
            chunk = turn - LAG
            pair_copy(chunk).wait_recv()
            summed = own[chunk] + pair_in[chunk].astype(F32)
            own[chunk] = summed
            line_out[chunk] = summed.astype(BF16)
            for step in range(1, line):
                line_copy(chunk, step).start()

        return carry

    lax.fori_loop(0, chunks + LAG, visit, 0)

    def finish(chunk, square_sum):
        for step in range(1, line):
            line_copy(chunk, step).wait_recv()
        summed = own[chunk, place]
        for step in range(1, line):
            summed += line_in[chunk, step - 1].astype(F32)
        final[chunk] = summed
        return square_sum + jnp.sum(summed * summed, axis=1, keepdims=True)

    square_sum = lax.fori_loop(0, chunks, finish, jnp.zeros((out_rows, 1), F32))
    squares[0] = jnp.broadcast_to(square_sum, squares.shape[1:])

    def square_copy(step):
        return remote(
            squares.at[0],
            squares.at[step],
            square_send.at[step - 1],
            square_recv.at[step - 1],
            section,
            (tensor + step) % tensors,
        )

    for step in range(1, tensors):
        square_copy(step).start()
    for step in range(1, tensors):
        square_copy(step).wait_recv()
    square_total = squares[0]
    for step in range(1, tensors):
        square_total += squares[step]
    inverse_rms = lax.rsqrt(square_total[:, 0:1] / (chunks * width * tensors) + 1e-05)
    for chunk in range(chunks):
        columns = slice(chunk * width, (chunk + 1) * width)
        gain = gain_ref[:, columns].astype(F32)
        out_ref[:, columns] = (final[chunk] * inverse_rms * gain).astype(BF16)

    for step in range(1, tensors):
        square_copy(step).wait_send()
    for group, root in enumerate(roots):

        @pl.when(section == root)
        def _(group=group):
            for step in range(1, sections):
                root_copy(group, step).wait_send()

        for step in range(1, half):
            row_copy(group, step).wait_send()
        for step in range(half):
            core_copy(group, step).wait_send()

    def drain(chunk, carry):
        pair_copy(chunk).wait_send()
        for step in range(1, line):
            line_copy(chunk, step).wait_send()
        return carry

    lax.fori_loop(0, chunks, drain, 0)


def merge(captured, weight, gain, sections, tensors):
    rows = captured.shape[0]
    groups, block, columns = weight.shape
    width = min(512, columns)
    chunks = columns // width
    row_total = rows * tensors
    out_rows = row_total // sections
    line = sections // 2
    half = tensors // 2
    dma = pltpu.SemaphoreType.DMA
    anywhere = pl.BlockSpec(memory_space=pl.ANY)
    vmem = pl.BlockSpec(memory_space=pltpu.VMEM)
    return pl.pallas_call(
        functools.partial(merge_kernel, sections, tensors),
        out_shape=jax.ShapeDtypeStruct((out_rows, columns), BF16),
        in_specs=[anywhere, anywhere, vmem],
        out_specs=vmem,
        scratch_shapes=[
            pltpu.VMEM((chunks, groups, block, width), BF16),
            pltpu.VMEM((groups, row_total, block), BF16),
            pltpu.VMEM((line, 2, out_rows, width), F32),
            pltpu.VMEM((chunks, line, out_rows, width), F32),
            pltpu.VMEM((chunks, line, out_rows, width), BF16),
            pltpu.VMEM((chunks, line, out_rows, width), BF16),
            pltpu.VMEM((chunks, line, out_rows, width), BF16),
            pltpu.VMEM((chunks, line - 1, out_rows, width), BF16),
            pltpu.VMEM((chunks, out_rows, width), F32),
            pltpu.VMEM((tensors, out_rows, 128), F32),
            dma((chunks,)),
            dma,
            dma((sections - 1,)),
            dma((groups,)),
            dma((groups, max(half - 1, 1))),
            dma((groups, max(half - 1, 1))),
            dma((groups, half)),
            dma((groups, half)),
            dma((chunks,)),
            dma((chunks,)),
            dma((chunks, line - 1)),
            dma((chunks, line - 1)),
            dma((tensors - 1,)),
            dma((tensors - 1,)),
        ],
        compiler_params=pltpu.CompilerParams(
            collective_id=0, has_side_effects=True, vmem_limit_bytes=61 * 2**20
        ),
        name="merge_layers",
    )(captured, weight, gain)


def solution(mesh):
    sections, tensors = mesh.shape["section"], mesh.shape["tensor"]

    def local(
        tree_queries,
        tree_kv,
        cache_kv,
        residual,
        cache_lengths,
        tree_parents,
        accepted,
        merging_weight,
        merging_gain,
    ):
        verified, captured = attend(
            tree_queries[0],
            tree_kv[0],
            cache_kv[0],
            residual[0],
            cache_lengths,
            tree_parents,
            accepted,
        )
        merged = merge(captured, merging_weight, merging_gain[None, :], sections, tensors)
        tokens = tree_queries.shape[2]
        return verified[None], merged.reshape(-1, tokens, merged.shape[1])

    return jax.shard_map(
        local,
        mesh=mesh,
        in_specs=(
            P("section", "tensor", None, None),
            P("section", "tensor", None, None, None),
            P("section", "tensor", None, None, None),
            P("section", "tensor", None, None),
            P("tensor"),
            P("tensor", None),
            P("tensor"),
            P(None, "section", "tensor"),
            P("tensor"),
        ),
        out_specs=(P("section", "tensor", None, None), P("section", None, "tensor")),
        check_vma=False,
    )
```

time: 228 us -> 79.2 us (0.35)
  waiting for transfers between devices: 82 us -> 0 us
  Pallas kernels: 0 us -> 68.3 us
  matrix products: 59.3 us -> 0 us
  blocking collectives: 28.7 us -> 0 us
  other arithmetic: 18.1 us -> 0 us
  between operations: 14.9 us -> 0.72 us
  local copies, waits for them, and re-layouts: 22.7 us -> 9.9 us
    pallas_call x0 -> x2, Pallas kernels: none -> 68.3 us  [the longest x1 59.7 us: merge(): pl.pallas_call(functools.partial(merge_kernel, sections, tensors), out_sh...]
    reduce_scatter x1 -> x0, waiting for transfers between devices: 63.4 us -> none  [local(): lax.psum_scatter(jnp.dot(gathered, local_weight, preferred_element_type=j...]
    dot_general x15 -> x0, matrix products: 59.3 us -> none  [the longest x1 20.6 us: local(): jnp.dot(gathered, local_weight, preferred_element_type=jnp.float32)]
    all_to_all x1 -> x0, blocking collectives: 23 us -> none  [feature_block(): lax.all_to_all(outgoing, 'section', split_axis=1, concat_axis=1, tiled=True)]
    all_gather x1 -> x0, waiting for transfers between devices: 18.6 us -> none  [local(): gathered = lax.all_gather(column_block, 'tensor', axis=0, tiled=True)]
    slice x7 -> x0, local copies, waits for them, and re-layouts: 7.03 us -> none  [the longest x6 6.45 us: visit(): window[:, :, 1].reshape(row_count, key_span, KV_HEADS, HEAD_DIM)]
    reduce_sum x8 -> x0, other arithmetic: 7 us -> none  [the longest x6 5.42 us: visit(): new_sum = old_sum * rescale + jnp.sum(block_weights, axis=-1)]
    psum x1 -> x0, blocking collectives: 5.66 us -> none  [local(): squares = lax.psum(jnp.sum(own_rows * own_rows, axis=1), 'tensor')]
  transfers between devices with their start and end apart: 2 -> 0, of which waited for: 2 -> 0; matrix products, arithmetic and copies ran while one was open for 2% -> 0% of each run, Pallas kernels for 0% -> 0%
where the time goes in v1:
time: 79.2 us; the launch traced here: 78.9 us
  Pallas kernels  68.3 us (86%)
  local copies, waits for them, and re-layouts  9.9 us (12%)
    pallas_call x1, Pallas kernels, merge(): pl.pallas_call(functools.partial(merge_kernel, sections, tensors), out_sh...  59.7 us
    pallas_call x1, Pallas kernels, attend(): pl.pallas_call(attention_kernel, grid=(rows,), out_shape=(jax.ShapeDtypeS...  8.59 us
    another operation x1, local copies, waits for them, and re-layouts, attend(): cache_kv.reshape(rows, cached, kv_width)  4.1 us
    unnamed x17, local copies, waits for them, and re-layouts  3.52 us
    reshape x1, local copies, waits for them, and re-layouts, local(): return (verified[None], merged.reshape(-1, tokens, merged.shape[1]))  1.62 us

profile of v1, /device:TPU:0, one launch (start us, length us, event | category | flops | bytes accessed | tf_op | source)
XLA Modules:
  0.0 78.9 jit_solution(1765984581331654426)
XLA Ops:
  0.6 0.0 copy-start.5
  0.6 0.0 copy-start.7
  0.7 0.0 copy-start.3
  0.7 0.0 copy-start.4
  0.7 4.1 %reshape_squeeze.6.cache_ref = bf16[8,192,1024]{2,1,0:T(8,128)(2,1)S(1)} reshape(bf16[1,8,96,2,1024]{4,3,2,1,0:T(2,128)(2,1)} %param.11) | data formatting | bytes 6291456 | tf_op jit(solution)/shard_map/reshape;squeeze | solution.py:156
  4.8 0.0 copy-done.5
  4.8 0.0 copy-start.6
  4.8 0.1 reshape_squeeze.7.tree_ref
  4.9 0.0 copy-done.7
  4.9 0.1 copy.11.parents_ref
  5.0 0.0 copy-done.3
  5.0 0.0 copy-done.4
  5.0 0.0 copy-start
  5.0 1.2 %copy-done = bf16[1,8,4,16384]{3,2,1,0:T(4,128)(2,1)S(1)} copy-done((bf16[1,8,4,16384]{3,2,1,0:T(4,128)(2,1)S(1)}, bf16[1,8,4,16384]{3,2,1,0:T(4,128)(2,1)}, u32[]{:S(2)}) %copy-start) | copy-done | bytes 1048600
  6.2 0.0 copy-start.1
  6.2 1.2 %copy-done.1 = bf16[1,8,4,16384]{3,2,1,0:T(4,128)(2,1)S(1)} copy-done((bf16[1,8,4,16384]{3,2,1,0:T(4,128)(2,1)S(1)}, bf16[1,8,4,16384]{3,2,1,0:T(4,128)(2,1)}, u32[]{:S(2)}) %copy-start.1) | copy-done | bytes 1048600
  7.4 8.6 %tree_attention.1 = (bf16[8,4,16384]{2,1,0:T(4,128)(2,1)}, bf16[32,16384]{1,0:T(8,128)(2,1)S(1)}) custom-call(s32[8]{0:T(128)S(1)} %copy-done.3, s32[8,4]{1,0:T(8,128)S(1)} %copy.11.parents_ref, s32[8]{0:T(128)S(1)} %copy-done.4, bf16[8,4,16384]{2,1,0:T(4,128)(2,1)S(1)} %bitcast.3, bf16[8,192,1024]{2,1,0:T(8,128)(2,1)S(1)} %reshape_squeeze.6.cache_ref, ...), custom_call_target="tpu_custom_call" | custom-call | tf_op jit(solution)/shard_map/tree_attention/pallas_call | solution.py:123
  16.0 0.0 copy-start.2
  16.0 1.0 %copy-done.2 = bf16[32,16384]{1,0:T(8,128)(2,1)} copy-done((bf16[32,16384]{1,0:T(8,128)(2,1)}, bf16[32,16384]{1,0:T(8,128)(2,1)S(1)}, u32[]{:S(2)}) %copy-start.2) | copy-done | bytes 1048600
  17.0 0.0 copy-done.6
  17.0 0.6 broadcast_in_dim.7.gain_ref
  17.6 59.7 %merge_layers.1 = bf16[16,4096]{1,0:T(8,128)(2,1)} custom-call(bf16[32,16384]{1,0:T(8,128)(2,1)} %copy-done.2, bf16[3,2048,4096]{2,1,0:T(8,128)(2,1)} %weight_ref.1, bf16[1,4096]{1,0:T(2,128)(2,1)} %broadcast_in_dim.7.gain_ref), custom_call_target="tpu_custom_call" | custom-call | tf_op jit(solution)/shard_map/merge_layers/pallas_call | solution.py:429
  77.3 1.6 %reshape.7 = bf16[4,4,4096]{2,1,0:T(4,128)(2,1)} reshape(bf16[16,4096]{1,0:T(8,128)(2,1)} %merge_layers.1) | data formatting | bytes 262144 | tf_op jit(solution)/shard_map/reshape | solution.py:492
Async XLA Ops:
  0.6 4.1 %copy-start.5 = (bf16[1,8,4,2,1024]{4,3,2,1,0:T(2,128)(2,1)S(1)}, bf16[1,8,4,2,1024]{4,3,2,1,0:T(2,128)(2,1)}, u32[]{:S(2)}) copy-start(bf16[1,8,4,2,1024]{4,3,2,1,0:T(2,128)(2,1)} %param.10) | copy-start | bytes 393220
  0.6 4.2 %copy-start.7 = (s32[8,4]{0,1:T(4,128)S(1)}, s32[8,4]{0,1:T(4,128)}, u32[]{:S(2)}) copy-start(s32[8,4]{0,1:T(4,128)} %param.14) | copy-start | bytes 388
  0.7 4.3 %copy-start.3 = (s32[8]{0:T(128)S(1)}, s32[8]{0:T(128)}, u32[]{:S(2)}) copy-start(s32[8]{0:T(128)} %lengths_ref.1) | copy-start | bytes 100
  0.7 4.3 %copy-start.4 = (s32[8]{0:T(128)S(1)}, s32[8]{0:T(128)}, u32[]{:S(2)}) copy-start(s32[8]{0:T(128)} %accepted_ref.1) | copy-start | bytes 100
  4.8 12.2 %copy-start.6 = (bf16[4096]{0:T(1024)(128)(2,1)S(1)}, bf16[4096]{0:T(1024)(128)(2,1)}, u32[]{:S(2)}) copy-start(bf16[4096]{0:T(1024)(128)(2,1)} %param.17) | copy-start | bytes 24580
  5.0 1.2 %copy-start = (bf16[1,8,4,16384]{3,2,1,0:T(4,128)(2,1)S(1)}, bf16[1,8,4,16384]{3,2,1,0:T(4,128)(2,1)}, u32[]{:S(2)}) copy-start(bf16[1,8,4,16384]{3,2,1,0:T(4,128)(2,1)} %param.9) | copy-start | bytes 3145732
  6.2 1.2 %copy-start.1 = (bf16[1,8,4,16384]{3,2,1,0:T(4,128)(2,1)S(1)}, bf16[1,8,4,16384]{3,2,1,0:T(4,128)(2,1)}, u32[]{:S(2)}) copy-start(bf16[1,8,4,16384]{3,2,1,0:T(4,128)(2,1)} %param.12) | copy-start | bytes 3145732
  16.0 1.0 %copy-start.2 = (bf16[32,16384]{1,0:T(8,128)(2,1)}, bf16[32,16384]{1,0:T(8,128)(2,1)S(1)}, u32[]{:S(2)}) copy-start(bf16[32,16384]{1,0:T(8,128)(2,1)S(1)} %get-tuple-element.5.captured_ref) | copy-start | bytes 3145732

commit v2 on v1

--- a/solution.py
+++ b/solution.py
@@ -146,7 +146,7 @@
             pltpu.VMEM((tokens, width), F32),
             pltpu.VMEM((rows * tokens // 8, 8, width), F32),
         ],
-        compiler_params=pltpu.CompilerParams(vmem_limit_bytes=32 * 2**20),
+        compiler_params=pltpu.CompilerParams(vmem_limit_bytes=61 * 2**20),
         name="tree_attention",
     )(
         lengths,
@@ -160,6 +160,7 @@
 
 
 LAG = 2
+PARTS = 2
 
 
 def merge_kernel(
@@ -199,11 +200,16 @@
     chunks, groups, block, width = weight_v.shape
     rows = captured_ref.shape[0]
     line = sections // 2
-    out_rows = out_ref.shape[0]
+    out_rows, tokens = sums.shape[2], out_ref.shape[1]
     place, parity = section // 2, section % 2
     partner = section + 1 - 2 * parity
     other_core = tensor + 1 - 2 * (tensor % 2)
-    roots = (0, sections // 2, sections - 1)
+    part_rows = rows // PARTS
+    flip = (2 * place) // line
+    order = [turn + flip * (groups - 1 - 2 * turn) for turn in range(groups)]
+
+    def root_of(group):
+        return group * (sections // 2) - group // 2
 
     def remote(src, dst, send, recv, to_section, to_tensor):
         return pltpu.make_async_remote_copy(
@@ -221,9 +227,6 @@
             weight_ref.at[:, :, columns], weight_v.at[chunk], weight_sem.at[chunk]
         )
 
-    for chunk in range(chunks):
-        weight_copy(chunk).start()
-
     barrier = pltpu.get_barrier_semaphore()
     for step in range(1, sections):
         pl.semaphore_signal(
@@ -235,76 +238,91 @@
         )
     pl.semaphore_wait(barrier, sections + tensors - 2)
 
-    def piece(group, owner):
-        return captured_v.at[group, pl.ds(pl.multiple_of(owner * rows, rows), rows), :]
-
-    def features(to_section):
-        return captured_ref.at[:, pl.ds(pl.multiple_of(to_section * block, block), block)]
-
-    def root_copy(group, step):
+    def piece(group, owner, part):
+        first = pl.multiple_of(owner * rows + part * part_rows, part_rows)
+        return captured_v.at[group, pl.ds(first, part_rows), :]
+
+    def features(to_section, part):
+        return captured_ref.at[
+            pl.ds(part * part_rows, part_rows),
+            pl.ds(pl.multiple_of(to_section * block, block), block),
+        ]
+
+    def root_copy(group, part, step):
         to_section = (section + step) % sections
         return remote(
-            features(to_section),
-            piece(group, tensor),
-            root_send.at[step - 1],
-            root_recv.at[group],
+            features(to_section, part),
+            piece(group, tensor, part),
+            root_send.at[part, step - 1],
+            root_recv.at[group, part],
             to_section,
             tensor,
         )
 
-    def root_local(group):
-        return pltpu.make_async_copy(features(section), piece(group, tensor), local_sem)
-
-    for group, root in enumerate(roots):
-
-        @pl.when(section == root)
+    def root_local(group, part):
+        return pltpu.make_async_copy(
+            features(section, part), piece(group, tensor, part), local_sem.at[part]
+        )
+
+    for group in range(groups):
+
+        @pl.when(section == root_of(group))
         def _(group=group):
-            for step in range(1, sections):
-                root_copy(group, step).start()
-            root_local(group).start()
-
-    def row_copy(group, step):
+            for part in range(PARTS):
+                for step in range(1, sections):
+                    root_copy(group, part, step).start()
+                root_local(group, part).start()
+
+    for chunk in range(chunks // 2):
+        weight_copy(chunk).start()
+
+    def row_copy(group, part, step):
         return remote(
-            piece(group, tensor),
-            piece(group, tensor),
-            row_send.at[group, step - 1],
-            row_recv.at[group, step - 1],
+            piece(group, tensor, part),
+            piece(group, tensor, part),
+            row_send.at[group, part, step - 1],
+            row_recv.at[group, part, step - 1],
             section,
             (tensor + 2 * step) % tensors,
         )
 
-    def core_copy(group, step):
+    def core_copy(group, part, step):
         owner = (tensor + tensors - 2 * step) % tensors
         return remote(
-            piece(group, owner),
-            piece(group, owner),
-            core_send.at[group, step],
-            core_recv.at[group, step],
+            piece(group, owner, part),
+            piece(group, owner, part),
+            core_send.at[group, part, step],
+            core_recv.at[group, part, step],
             section,
             other_core,
         )
 
     half = tensors // 2
-    for group, root in enumerate(roots):
-
-        @pl.when(section == root)
-        def _(group=group):
-            root_local(group).wait()
-
-        @pl.when(section != root)
-        def _(group=group):
-            root_copy(group, 1).wait_recv()
-
-        for step in range(1, half):
-            row_copy(group, step).start()
-        core_copy(group, 0).start()
-    for group in range(groups):
-        for step in range(1, half):
-            row_copy(group, step).wait_recv()
-            core_copy(group, step).start()
-    for group in range(groups):
-        for step in range(half):
-            core_copy(group, step).wait_recv()
+    for part in range(PARTS):
+        for group in order:
+
+            @pl.when(section == root_of(group))
+            def _(group=group, part=part):
+                root_local(group, part).wait()
+
+            @pl.when(section != root_of(group))
+            def _(group=group, part=part):
+                root_copy(group, part, 1).wait_recv()
+
+            for step in range(1, half):
+                row_copy(group, part, step).start()
+            core_copy(group, part, 0).start()
+    for chunk in range(chunks // 2, chunks):
+        weight_copy(chunk).start()
+    for part in range(PARTS):
+        for group in order:
+            for step in range(1, half):
+                row_copy(group, part, step).wait_recv()
+                core_copy(group, part, step).start()
+    for part in range(PARTS):
+        for group in order:
+            for step in range(half):
+                core_copy(group, part, step).wait_recv()
 
     def pair_copy(chunk):
         return remote(
@@ -389,21 +407,25 @@
     for chunk in range(chunks):
         columns = slice(chunk * width, (chunk + 1) * width)
         gain = gain_ref[:, columns].astype(F32)
-        out_ref[:, columns] = (final[chunk] * inverse_rms * gain).astype(BF16)
+        normed = (final[chunk] * inverse_rms * gain).astype(BF16)
+        for row in range(out_rows // tokens):
+            out_ref[row, :, columns] = normed[row * tokens : (row + 1) * tokens]
 
     for step in range(1, tensors):
         square_copy(step).wait_send()
-    for group, root in enumerate(roots):
-
-        @pl.when(section == root)
+    for group in range(groups):
+
+        @pl.when(section == root_of(group))
         def _(group=group):
-            for step in range(1, sections):
-                root_copy(group, step).wait_send()
-
-        for step in range(1, half):
-            row_copy(group, step).wait_send()
-        for step in range(half):
-            core_copy(group, step).wait_send()
+            for part in range(PARTS):
+                for step in range(1, sections):
+                    root_copy(group, part, step).wait_send()
+
+        for part in range(PARTS):
+            for step in range(1, half):
+                row_copy(group, part, step).wait_send()
+            for step in range(half):
+                core_copy(group, part, step).wait_send()
 
     def drain(chunk, carry):
         pair_copy(chunk).wait_send()
@@ -414,7 +436,7 @@
     lax.fori_loop(0, chunks, drain, 0)
 
 
-def merge(captured, weight, gain, sections, tensors):
+def merge(captured, weight, gain, sections, tensors, tokens):
     rows = captured.shape[0]
     groups, block, columns = weight.shape
     width = min(512, columns)
@@ -428,7 +450,7 @@
     vmem = pl.BlockSpec(memory_space=pltpu.VMEM)
     return pl.pallas_call(
         functools.partial(merge_kernel, sections, tensors),
-        out_shape=jax.ShapeDtypeStruct((out_rows, columns), BF16),
+        out_shape=jax.ShapeDtypeStruct((out_rows // tokens, tokens, columns), BF16),
         in_specs=[anywhere, anywhere, vmem],
         out_specs=vmem,
         scratch_shapes=[
@@ -443,13 +465,13 @@
             pltpu.VMEM((chunks, out_rows, width), F32),
             pltpu.VMEM((tensors, out_rows, 128), F32),
             dma((chunks,)),
-            dma,
-            dma((sections - 1,)),
-            dma((groups,)),
-            dma((groups, max(half - 1, 1))),
-            dma((groups, max(half - 1, 1))),
-            dma((groups, half)),
-            dma((groups, half)),
+            dma((PARTS,)),
+            dma((PARTS, sections - 1)),
+            dma((groups, PARTS)),
+            dma((groups, PARTS, max(half - 1, 1))),
+            dma((groups, PARTS, max(half - 1, 1))),
+            dma((groups, PARTS, half)),
+            dma((groups, PARTS, half)),
             dma((chunks,)),
             dma((chunks,)),
             dma((chunks, line - 1)),
@@ -487,9 +509,11 @@
             tree_parents,
             accepted,
         )
-        merged = merge(captured, merging_weight, merging_gain[None, :], sections, tensors)
         tokens = tree_queries.shape[2]
-        return verified[None], merged.reshape(-1, tokens, merged.shape[1])
+        draft_input = merge(
+            captured, merging_weight, merging_gain[None, :], sections, tensors, tokens
+        )
+        return verified[None], draft_input
 
     return jax.shard_map(
         local,

time: 79.2 us -> 74.9 us (0.946)
  Pallas kernels: 68.3 us -> 64.4 us
    pallas_call x1, Pallas kernels: 59.7 us -> 54.2 us  [merge(): pl.pallas_call(functools.partial(merge_kernel, sections, tensors), out_sh...]
    another operation x1, local copies, waits for them, and re-layouts: 4.1 us -> 5.78 us  [attend(): cache_kv.reshape(rows, cached, kv_width)]
    pallas_call x1, Pallas kernels: 8.59 us -> 10.3 us  [attend(): pl.pallas_call(attention_kernel, grid=(rows,), out_shape=(jax.ShapeDtypeS...]
    reshape x1 -> x0, local copies, waits for them, and re-layouts: 1.62 us -> none  [local(): return (verified[None], merged.reshape(-1, tokens, merged.shape[1]))]
    unnamed x17 -> x8, local copies, waits for them, and re-layouts: 3.52 us -> 2.28 us
where the time goes in v2:
time: 74.9 us; the launch traced here: 74.5 us
  Pallas kernels  64.4 us (86%)
  local copies, waits for them, and re-layouts  9.38 us (13%)
    pallas_call x1, Pallas kernels, merge(): pl.pallas_call(functools.partial(merge_kernel, sections, tensors), out_sh...  54.2 us
    pallas_call x1, Pallas kernels, attend(): pl.pallas_call(attention_kernel, grid=(rows,), out_shape=(jax.ShapeDtypeS...  10.3 us
    another operation x1, local copies, waits for them, and re-layouts, attend(): cache_kv.reshape(rows, cached, kv_width)  5.78 us
    unnamed x8, local copies, waits for them, and re-layouts  2.28 us

profile of v2, /device:TPU:0, one launch (start us, length us, event | category | flops | bytes accessed | tf_op | source)
XLA Modules:
  0.0 74.5 jit_solution(12525356173304240078)
XLA Ops:
  0.6 0.0 copy-start
  0.6 0.0 copy-start.2
  0.7 5.8 %reshape_squeeze.6.cache_ref = bf16[8,192,1024]{2,1,0:T(8,128)(2,1)} reshape(bf16[1,8,96,2,1024]{4,3,2,1,0:T(2,128)(2,1)} %param.11) | data formatting | bytes 6291456 | tf_op jit(solution)/shard_map/reshape;squeeze | solution.py:156
  6.4 0.0 copy-done
  6.4 0.0 copy-start.1
  6.4 0.7 reshape_squeeze.7.tree_ref
  7.1 0.0 copy-done.2
  7.1 0.7 copy.11.parents_ref
  7.8 10.3 %tree_attention.1 = (bf16[8,4,16384]{2,1,0:T(4,128)(2,1)}, bf16[32,16384]{1,0:T(8,128)(2,1)}) custom-call(s32[8]{0:T(128)} %lengths_ref.1, s32[8,4]{1,0:T(8,128)} %copy.11.parents_ref, s32[8]{0:T(128)} %accepted_ref.1, bf16[8,4,16384]{2,1,0:T(4,128)(2,1)} %bitcast.3, bf16[8,192,1024]{2,1,0:T(8,128)(2,1)} %reshape_squeeze.6.cache_ref, ...), custom_call_target="tpu_custom_call" | custom-call | tf_op jit(solution)/shard_map/tree_attention/pallas_call | solution.py:123
  18.1 0.0 copy-done.1
  18.1 0.6 broadcast_in_dim.7.gain_ref
  18.7 54.2 %merge_layers.1 = bf16[4,4,4096]{2,1,0:T(4,128)(2,1)} custom-call(bf16[32,16384]{1,0:T(8,128)(2,1)} %get-tuple-element.5.captured_ref, bf16[3,2048,4096]{2,1,0:T(8,128)(2,1)} %weight_ref.1, bf16[1,4096]{1,0:T(2,128)(2,1)} %broadcast_in_dim.7.gain_ref), custom_call_target="tpu_custom_call" | custom-call | tf_op jit(solution)/shard_map/merge_layers/pallas_call | solution.py:451
  72.9 1.6 %copy.13 = bf16[4,4,4096]{2,1,0:T(4,128)(2,1)} copy(bf16[4,4,4096]{2,1,0:T(4,128)(2,1)} %merge_layers.1) | data formatting | bytes 262144
Async XLA Ops:
  0.6 5.8 %copy-start = (bf16[1,8,4,2,1024]{4,3,2,1,0:T(2,128)(2,1)S(1)}, bf16[1,8,4,2,1024]{4,3,2,1,0:T(2,128)(2,1)}, u32[]{:S(2)}) copy-start(bf16[1,8,4,2,1024]{4,3,2,1,0:T(2,128)(2,1)} %param.10) | copy-start | bytes 393220
  0.6 6.5 %copy-start.2 = (s32[8,4]{0,1:T(4,128)S(1)}, s32[8,4]{0,1:T(4,128)}, u32[]{:S(2)}) copy-start(s32[8,4]{0,1:T(4,128)} %param.14) | copy-start | bytes 388
  6.4 11.6 %copy-start.1 = (bf16[4096]{0:T(1024)(128)(2,1)S(1)}, bf16[4096]{0:T(1024)(128)(2,1)}, u32[]{:S(2)}) copy-start(bf16[4096]{0:T(1024)(128)(2,1)} %param.17) | copy-start | bytes 24580

commit v3 on v2

--- a/solution.py
+++ b/solution.py
@@ -180,6 +180,7 @@
     line_in,
     final,
     squares,
+    partial,
     weight_sem,
     local_sem,
     root_send,
@@ -314,15 +315,26 @@
             core_copy(group, part, 0).start()
     for chunk in range(chunks // 2, chunks):
         weight_copy(chunk).start()
-    for part in range(PARTS):
-        for group in order:
+    for turn, group in enumerate(order):
+        for part in range(PARTS):
             for step in range(1, half):
                 row_copy(group, part, step).wait_recv()
                 core_copy(group, part, step).start()
-    for part in range(PARTS):
-        for group in order:
+        for part in range(PARTS):
             for step in range(half):
                 core_copy(group, part, step).wait_recv()
+        if turn < groups - 1:
+
+            def accumulate(chunk, carry, turn=turn, group=group):
+                if turn == 0:
+                    weight_copy(chunk).wait()
+                product = jnp.dot(
+                    captured_v[group], weight_v[chunk, group], preferred_element_type=F32
+                )
+                partial[chunk] = product if turn == 0 else partial[chunk] + product
+                return carry
+
+            lax.fori_loop(0, chunks, accumulate, 0)
 
     def pair_copy(chunk):
         return remote(
@@ -349,12 +361,10 @@
         @pl.when(turn < chunks)
         def _():
             chunk = turn
-            weight_copy(chunk).wait()
-            product = jnp.dot(captured_v[0], weight_v[chunk, 0], preferred_element_type=F32)
-            for group in range(1, groups):
-                product += jnp.dot(
-                    captured_v[group], weight_v[chunk, group], preferred_element_type=F32
-                )
+            group = order[-1]
+            product = partial[chunk] + jnp.dot(
+                captured_v[group], weight_v[chunk, group], preferred_element_type=F32
+            )
             sums[...] = product.reshape(line, 2, out_rows, width)
             own[chunk] = sums[:, parity]
             pair_out[chunk] = sums[:, 1 - parity].astype(BF16)
@@ -464,6 +474,7 @@
             pltpu.VMEM((chunks, line - 1, out_rows, width), BF16),
             pltpu.VMEM((chunks, out_rows, width), F32),
             pltpu.VMEM((tensors, out_rows, 128), F32),
+            pltpu.VMEM((chunks, row_total, width), F32),
             dma((chunks,)),
             dma((PARTS,)),
             dma((PARTS, sections - 1)),

time: 74.9 us -> 84.5 us (1.13)
  Pallas kernels: 64.4 us -> 74 us
    pallas_call x1, Pallas kernels: 54.2 us -> 63.7 us  [merge(): pl.pallas_call(functools.partial(merge_kernel, sections, tensors), out_sh...]
where the time goes in v3:
time: 84.5 us; the launch traced here: 84 us
  Pallas kernels  74 us (88%)
  local copies, waits for them, and re-layouts  9.38 us (11%)
    pallas_call x1, Pallas kernels, merge(): pl.pallas_call(functools.partial(merge_kernel, sections, tensors), out_sh...  63.7 us
    pallas_call x1, Pallas kernels, attend(): pl.pallas_call(attention_kernel, grid=(rows,), out_shape=(jax.ShapeDtypeS...  10.3 us
    another operation x1, local copies, waits for them, and re-layouts, attend(): cache_kv.reshape(rows, cached, kv_width)  5.78 us
    unnamed x8, local copies, waits for them, and re-layouts  2.28 us

profile of v3, /device:TPU:0, one launch (start us, length us, event | category | flops | bytes accessed | tf_op | source)
XLA Modules:
  0.0 84.0 jit_solution(10971414467322920065)
XLA Ops:
  0.6 0.0 copy-start
  0.6 0.0 copy-start.2
  0.7 5.8 %reshape_squeeze.6.cache_ref = bf16[8,192,1024]{2,1,0:T(8,128)(2,1)} reshape(bf16[1,8,96,2,1024]{4,3,2,1,0:T(2,128)(2,1)} %param.11) | data formatting | bytes 6291456 | tf_op jit(solution)/shard_map/reshape;squeeze | solution.py:156
  6.4 0.0 copy-done
  6.4 0.0 copy-start.1
  6.4 0.7 reshape_squeeze.7.tree_ref
  7.1 0.0 copy-done.2
  7.1 0.7 copy.11.parents_ref
  7.8 10.3 %tree_attention.1 = (bf16[8,4,16384]{2,1,0:T(4,128)(2,1)}, bf16[32,16384]{1,0:T(8,128)(2,1)}) custom-call(s32[8]{0:T(128)} %lengths_ref.1, s32[8,4]{1,0:T(8,128)} %copy.11.parents_ref, s32[8]{0:T(128)} %accepted_ref.1, bf16[8,4,16384]{2,1,0:T(4,128)(2,1)} %bitcast.3, bf16[8,192,1024]{2,1,0:T(8,128)(2,1)} %reshape_squeeze.6.cache_ref, ...), custom_call_target="tpu_custom_call" | custom-call | tf_op jit(solution)/shard_map/tree_attention/pallas_call | solution.py:123
  18.1 0.0 copy-done.1
  18.1 0.6 broadcast_in_dim.7.gain_ref
  18.7 63.7 %merge_layers.1 = bf16[4,4,4096]{2,1,0:T(4,128)(2,1)} custom-call(bf16[32,16384]{1,0:T(8,128)(2,1)} %get-tuple-element.5.captured_ref, bf16[3,2048,4096]{2,1,0:T(8,128)(2,1)} %weight_ref.1, bf16[1,4096]{1,0:T(2,128)(2,1)} %broadcast_in_dim.7.gain_ref), custom_call_target="tpu_custom_call" | custom-call | tf_op jit(solution)/shard_map/merge_layers/pallas_call | solution.py:461
  82.4 1.6 %copy.13 = bf16[4,4,4096]{2,1,0:T(4,128)(2,1)} copy(bf16[4,4,4096]{2,1,0:T(4,128)(2,1)} %merge_layers.1) | data formatting | bytes 262144
Async XLA Ops:
  0.6 5.8 %copy-start = (bf16[1,8,4,2,1024]{4,3,2,1,0:T(2,128)(2,1)S(1)}, bf16[1,8,4,2,1024]{4,3,2,1,0:T(2,128)(2,1)}, u32[]{:S(2)}) copy-start(bf16[1,8,4,2,1024]{4,3,2,1,0:T(2,128)(2,1)} %param.10) | copy-start | bytes 393220
  0.6 6.5 %copy-start.2 = (s32[8,4]{0,1:T(4,128)S(1)}, s32[8,4]{0,1:T(4,128)}, u32[]{:S(2)}) copy-start(s32[8,4]{0,1:T(4,128)} %param.14) | copy-start | bytes 388
  6.4 11.6 %copy-start.1 = (bf16[4096]{0:T(1024)(128)(2,1)S(1)}, bf16[4096]{0:T(1024)(128)(2,1)}, u32[]{:S(2)}) copy-start(bf16[4096]{0:T(1024)(128)(2,1)} %param.17) | copy-start | bytes 24580
